TPU v7x, 256 devices: a whole 4x4x8 slice. The times are simulated.
256 devices in a mesh: row: 32 (over y_lo, z, core), col: 8 (over x, y_hi).
Axes of the slice: x: 4, y: 4 (y_hi: 2, y_lo: 2; y = y_hi * 2 + y_lo), z: 8, core: 2. Of those that a mesh axis runs over, the one named last changes fastest.
Arguments:
- features: bfloat16 [32, 1024, 4096], P(None, 'row', 'col'), may hold values from -6 to 6
- mask: int32 [1024, 4096], P('row', 'col'), may hold values from 0 to 1, as said below
- mask_gain: float32 [32], replicated, may hold values from -3 to 3
- conv_one: bfloat16 [9, 32, 32], replicated, may hold values from -0.375 to 0.375
- conv_two: bfloat16 [9, 32, 32], replicated, may hold values from -0.375 to 0.375
- spec_real: bfloat16 [2048, 32, 32], P(('row', 'col')), may hold values from -5 to 5
- spec_imag: bfloat16 [2048, 32, 32], P(('row', 'col')), may hold values from -5 to 5
- cotangent: bfloat16 [32, 1024, 4096], P(None, 'row', 'col'), may hold values from -6 to 6
Outputs:
- output: bfloat16 [32, 1024, 4096], P(None, 'row', 'col')
- grad_conv_one: float32 [9, 32, 32], replicated
- grad_conv_two: float32 [9, 32, 32], replicated
- grad_spec_real: float32 [2048, 32, 32], P(('row', 'col'))
- grad_spec_imag: float32 [2048, 32, 32], P(('row', 'col'))
Inputs may be any that keep to these rules, and one draw needn't show every extreme that they name: `mask`: layout pixels, each exactly 0 or 1.
All inputs are finite; a program needn't handle non-finite values.
Results may differ from a plain program's by a relative error of at most 0.006.
Values may be sent and summed in bfloat16 or wider, within the bound.
A program may use at most 192 MiB of HBM per device.

v0:
```python
import functools
import math

import jax
import jax.numpy as jnp
import ml_dtypes
import numpy as np
from jax import lax
from jax.experimental import pallas as pl
from jax.experimental.pallas import tpu as pltpu
from jax.sharding import PartitionSpec as P

C = 32
M = 32
RATIO = 8
MESH = pl.DeviceIdType.MESH
HIGH = lax.Precision.HIGHEST
F32 = jnp.float32
BF16 = jnp.bfloat16
GELU_A = math.sqrt(2.0 / math.pi)
GELU_B = 0.044715
VMEM_LIMIT = 56 * 2**20
NT = (((1,), (1,)), ((), ()))
TN = (((0,), (0,)), ((), ()))
NN = (((1,), (0,)), ((), ()))


def dot(a, b, dims, precision=None):
    return lax.dot_general(a, b, dims, preferred_element_type=F32, precision=precision)


def weights_np():
    d = (np.arange(RATIO) + 0.5 - RATIO / 2) / RATIO
    return np.stack([np.maximum(-d, 0.0), 1.0 - np.abs(d), np.maximum(d, 0.0)])


def column_tables(n_col):
    w = weights_np()
    n_two = 64 * n_col
    r = np.arange(M)
    out = np.zeros((n_col, 2, 64, 512))
    for j in range(n_col):
        fine = np.arange(512)
        cell, s = 64 * j + fine // RATIO, fine % RATIO

        def wave(at):
            return np.exp(-2j * np.pi * ((r[:, None] * at[None, :]) % n_two) / n_two)

        mean = wave(cell) / 64.0
        restrict = sum(w[b + 1][s][None, :] * wave(cell + b) for b in (-1, 0, 1))
        for kind, value in enumerate((mean, restrict)):
            parts = np.stack([value.real, value.imag], axis=0).reshape(2, 4, 8, 512)
            out[j, kind] = parts.transpose(1, 0, 2, 3).reshape(64, 512)
    out = out.astype(np.float32)
    upper = out.astype(ml_dtypes.bfloat16)
    lower = (out - upper.astype(np.float32)).astype(ml_dtypes.bfloat16)
    return np.concatenate([upper, lower], axis=2)


def row_tables(n_row):
    n_z = n_row // 4
    peers = np.arange(n_row).reshape(2, n_z, 2).transpose(1, 0, 2).reshape(-1)
    n_one = 4 * n_row
    q_all = np.arange(2 * n_row)
    f1 = np.where(q_all < n_row, q_all, n_one - 2 * n_row + q_all)
    out = np.zeros((2 * n_row, n_row, 16))
    for i in range(n_row):
        for h in range(2):
            q = 2 * peers + h
            for kk in range(6):
                phase = 2 * np.pi * ((f1[q] * (4 * i + kk - 1)) % n_one) / n_one
                out[2 * i + h, :, 2 * kk] = np.cos(phase)
                out[2 * i + h, :, 2 * kk + 1] = np.sin(phase)
    out = out.reshape(2 * n_row, n_z, 64)
    return np.pad(out, ((0, 0), (0, 0), (0, 64))).astype(np.float32)


def prolong_table():
    w = weights_np()
    out = np.zeros((C, RATIO, 3, C))
    for c in range(C):
        out[c, :, :, c] = w.T
    return out.reshape(C * RATIO, 3 * C).astype(np.float32)


def turn_table():
    w = weights_np()
    sums = np.zeros((2, C, C, 16))
    turn = np.zeros((16, C, C, 16))
    restrict = np.zeros((4, C, C, 16))
    for c in range(C):
        for row in range(16):
            cell, p = row // RATIO, row % RATIO
            sums[cell, c, c, row] = 1.0
            turn[row, c, c, row] = 1.0
            for a in (-1, 0, 1):
                restrict[cell + a + 1, c, c, row] = w[a + 1][p]
    return np.concatenate([t.reshape(-1, C * 16) for t in (sums, turn, restrict)], axis=0).astype(np.float32)


def expand_table():
    return np.repeat(np.eye(C), RATIO, axis=0).astype(np.float32)


def lane_group(shape):
    return lax.broadcasted_iota(jnp.int32, shape, len(shape) - 1) // 32


def place(value, source, target):
    shift = (32 * (target - source)) % 128
    moved = pltpu.roll(value, shift, 1) if shift else value
    return jnp.where(lane_group(value.shape) == target, moved, 0.0)


def everywhere(value):
    value = value + pltpu.roll(value, 64, 1)
    return value + pltpu.roll(value, 32, 1)


def remote(src, dst, send, recv, row, col):
    return pltpu.make_async_remote_copy(
        src_ref=src,
        dst_ref=dst,
        send_sem=send,
        recv_sem=recv,
        device_id=(row, col),
        device_id_type=MESH,
    )


def remote_to(plan, send, recv):
    return [
        remote(src, dst, send.at[n], recv.at[n], row, col)
        for n, (src, dst, row, col) in enumerate(plan)
    ]


def begin(copies):
    for copy in copies:
        copy.start()


def arrive(copies):
    for copy in copies:
        copy.wait_recv()


def leave(copies):
    for copy in copies:
        copy.wait_send()


def prepare(feat, mask, gain, cot, turn, lext, cext, field, ready):
    for half in range(2):
        ready[half]()
        rows = slice(16 * half, 16 * half + 16)
        to = slice(4 + 16 * half, 20 + 16 * half)
        raised = mask[rows, :].astype(F32) - 0.5
        for c in range(C):
            feat[c, rows, :] = (feat[c, rows, :].astype(F32) + gain[c] * raised).astype(BF16)
        turned = dot(turn[0:576], feat[:, rows, :].reshape(512, 512), NN)
        field[2 * half : 2 * half + 2] = turned[0:64].reshape(2, 32, 512)
        lext[to, :, 0:512] = turned[64:576].astype(BF16).reshape(16, 32, 512)
        turned = dot(turn[64:704], cot[:, rows, :].reshape(512, 512), NN)
        cext[to, :, 0:512] = turned[0:512].astype(BF16).reshape(16, 32, 512)
        sums = turned[512:640].reshape(4, 32, 512)
        if half == 0:
            field[4:8] = sums
        else:
            field[6:8] = field[6:8] + sums[0:2]
            field[8:10] = sums[2:4]


def parts_of(value, count):
    out = []
    for _ in range(count):
        part = value.astype(BF16)
        out.append(part)
        value = value - part.astype(F32)
    return out


def transform(table, value):
    upper, lower = parts_of(value, 2)
    whole = dot(table, upper, NT)
    return whole[0:64] + whole[64:128] + dot(table[0:64], lower, NT)


def pick(shape, pairs):
    row = lax.broadcasted_iota(jnp.int32, shape, 0)
    lane = lax.broadcasted_iota(jnp.int32, shape, 1)
    hit = jnp.zeros(shape, jnp.bool_)
    for r, l in pairs:
        hit = hit | ((row == r) & (lane == l))
    return jnp.where(hit, 1.0, 0.0).astype(BF16)


def tiled(value):
    wide = jnp.concatenate([value, jnp.zeros((32, 96), value.dtype)], axis=1)
    return everywhere(wide)


def shifted(value, by):
    if by > 0:
        return jnp.concatenate([value[:, 640 - by :], value[:, : 640 - by]], axis=1)
    return jnp.concatenate([value[:, -by:], value[:, :-by]], axis=1)


def main_kernel(
    n_row, n_col, scaling, scale,
    feat_h, mask_h, gain, cot_h, real_h, imag_h, one_h, two_h, spread_h, stretch_h, turn_h, col_tab, row_tab,
    stage_out, total_out, outer_out,
    feat, mask, cot, w_real, w_imag, w_one, w_two, spread, stretch, turn, stage,
    lext, cext, high, low, field, tab, twiddle,
    share, share_in, part, part_z, quad_sum, part_q, quad, mixed_in, folded, folded_in,
    left, right, side_in, rows_in, row_c_in,
    l_shift, c_shift, h_shift, slope, band_one, band_two, band_tail, band_back, sum_one, sum_two,
    mine, sum_c, chunk_c, sum_q, chunk_q, sum_z, done, gathered,
    local_sem, halo_send, halo_recv, a_send, a_recv, bz_send, bz_recv, bq_send, bq_recv,
    cq_send, cq_recv, cz_send, cz_recv, d_send, d_recv,
    r_send, r_recv, rq_send, rq_recv, rz_send, rz_recv, g_send, g_recv,
):
    i = lax.axis_index("row")
    j = lax.axis_index("col")
    half = j // 4
    n_z = n_row // 4
    y, z, core = i // (2 * n_z), (i // 2) % n_z, i % 2
    quarter = 2 * y + core
    up, down = (i + n_row - 1) % n_row, (i + 1) % n_row
    west, east = (j + n_col - 1) % n_col, (j + 1) % n_col
    cols = [(j + d) % n_col for d in range(1, n_col)]
    levels = [(z + d) % n_z for d in range(1, n_z)]
    quarters = [(y, 1 - core), (1 - y, core), (1 - y, 1 - core)]

    def row_at(y, z, core):
        return (y * n_z + z) * 2 + core

    loads = [
        pltpu.make_async_copy(src, dst, local_sem.at[n])
        for n, (src, dst) in enumerate(
            (
                (mask_h, mask),
                (feat_h.at[:, 0:16], feat.at[:, 0:16]),
                (turn_h, turn),
                (cot_h.at[:, 0:16], cot.at[:, 0:16]),
                (feat_h.at[:, 16:32], feat.at[:, 16:32]),
                (cot_h.at[:, 16:32], cot.at[:, 16:32]),
                (col_tab.at[j], tab),
                (row_tab.at[2 * i + half], twiddle),
                (one_h, w_one),
                (two_h, w_two),
                (spread_h, spread),
                (stretch_h, stretch),
                (real_h, w_real),
                (imag_h, w_imag),
            )
        )
    ]
    begin(loads)

    barrier = pltpu.get_barrier_semaphore()
    partners = (
        [(i, c) for c in cols]
        + [(row_at(y, l, core), j) for l in levels]
        + [(row_at(a, z, b), j) for a, b in quarters]
        + [(r, c) for r in (up, down) for c in (j, west, east)]
    )
    for partner in partners:
        pl.semaphore_signal(barrier, inc=1, device_id=partner, device_id_type=MESH)

    def first_half():
        for load in loads[0:4]:
            load.wait()

    def second_half():
        for load in loads[4:6]:
            load.wait()

    prepare(feat, mask, gain, cot, turn, lext, cext, field, (first_half, second_half))

    loads[6].wait()
    share[:, 0:128] = transform(tab[0], field[0:4].reshape(128, 512))
    share[:, 128:320] = transform(tab[1], field[4:10].reshape(192, 512))
    share[:, 320:384] = jnp.zeros((64, 64), F32)
    pl.semaphore_wait(barrier, len(partners))

    def group(c):
        return pl.ds(pl.multiple_of(16 * (c % 4), 16), 16)

    a_copies = remote_to([(share.at[group(c)], share_in.at[j], i, c) for c in cols], a_send, a_recv)
    begin(a_copies)
    share_in[j] = share[group(j), :]

    first_l = lext[4:36, :, 0:128].reshape(1024, 128)
    last_l = lext[4:36, :, 384:512].reshape(1024, 128)
    first_c = cext[4:36, :, 0:128].reshape(1024, 128)
    last_c = cext[4:36, :, 384:512].reshape(1024, 128)
    sel = (16, 128)
    left[...] = (
        dot(pick(sel, ((0, 0), (1, 1))), first_l, NT) + dot(pick(sel, ((2, 0),)), first_c, NT)
    )[0:4]
    right[...] = (
        dot(pick(sel, ((0, 126), (1, 127))), last_l, NT) + dot(pick(sel, ((2, 127),)), last_c, NT)
    )[0:4]
    plan = [
        (lext.at[4:6, :, 0:512], rows_in.at[1], up, j),
        (lext.at[34:36, :, 0:512], rows_in.at[0], down, j),
        (cext.at[4:5, :, 0:512], row_c_in.at[1], up, j),
        (cext.at[35:36, :, 0:512], row_c_in.at[0], down, j),
        (left, side_in.at[1, :, 128:1152], i, west),
        (right, side_in.at[0, :, 128:1152], i, east),
        (left.at[:, 0:128], side_in.at[1, :, 1152:1280], up, west),
        (right.at[:, 0:128], side_in.at[0, :, 1152:1280], up, east),
        (left.at[:, 896:1024], side_in.at[1, :, 0:128], down, west),
        (right.at[:, 896:1024], side_in.at[0, :, 0:128], down, east),
    ]
    halos = remote_to(plan, halo_send, halo_recv)
    begin(halos)

    for load in loads[7:]:
        load.wait()
    eye = jnp.where(
        lax.broadcasted_iota(jnp.int32, (32, 32), 0) == lax.broadcasted_iota(jnp.int32, (32, 32), 1),
        1.0,
        0.0,
    ).astype(BF16)
    block = lane_group((32, 256))
    line = lax.broadcasted_iota(jnp.int32, (256, 384), 0) % 8
    wide_block = lane_group((256, 384))
    for v in range(3):
        ones, backs, twos = [], [], []
        for u in range(3):
            one = tiled(w_one[3 * u + v].astype(F32))
            ones.append(jnp.concatenate([one, one], axis=1))
            back = tiled(dot(eye, w_two[3 * u + v], NT))
            backs.append(jnp.concatenate([back, back], axis=1))
            two = tiled(w_two[3 * u + v].astype(F32))
            twos.append(jnp.concatenate([two, two, two], axis=1).astype(BF16))
        for r in range(6):
            one = jnp.zeros((32, 256), F32)
            back = jnp.zeros((32, 256), F32)
            for u in range(3):
                one = one + jnp.where(block == r + u, ones[u], 0.0)
                back = back + jnp.where(block == r + 2 - u, backs[u], 0.0)
            band_one[v, 32 * r : 32 * r + 32, :] = one.astype(BF16)
            band_back[v, 32 * r : 32 * r + 32, :] = back.astype(BF16)
        total = jnp.zeros((256, 384), F32)
        for u in range(3):
            total = total + jnp.where(
                wide_block - line == u, dot(spread[...], twos[u], NN), 0.0
            )
        band_two[v] = total[:, 0:256].astype(BF16)
        band_tail[:, 64 * v : 64 * v + 64] = total[:, 256:320].astype(BF16)
    band_tail[:, 192:288] = stretch[...]
    band_tail[:, 288:384] = stretch[...]

    arrive(halos)
    lext[2:4, :, 0:512] = rows_in[0]
    lext[36:38, :, 0:512] = rows_in[1]
    cext[3:4, :, 0:512] = row_c_in[0]
    cext[36:37, :, 0:512] = row_c_in[1]
    sides = jnp.concatenate([side_in[0], side_in[1]], axis=0).astype(BF16)
    at_l = pick((8, 128), ((0, 126), (1, 127), (4, 0), (5, 1)))
    at_c = pick((8, 128), ((2, 127), (6, 0)))
    lext[:, :, 512:640] = dot(sides, at_l, TN).astype(BF16).reshape(40, 32, 128)
    cext[:, :, 512:640] = dot(sides, at_c, TN).astype(BF16).reshape(40, 32, 128)

    def move(k):
        rows = pl.ds(2 + 4 * k, 4)
        value = lext[rows].reshape(128, 640)
        l_shift[0, rows] = shifted(value, 1).reshape(4, 32, 640)
        l_shift[1, rows] = shifted(value, -1).reshape(4, 32, 640)
        value = cext[rows].reshape(128, 640)
        c_shift[0, rows] = shifted(value, 1)[:, 0:512].reshape(4, 32, 512)
        c_shift[1, rows] = shifted(value, -1)[:, 0:512].reshape(4, 32, 512)

    for k in range(9):
        move(k)

    arrive(a_copies)
    total_a = share_in[0]
    for k in range(1, n_col):
        total_a = total_a + share_in[k]
    ps, qs = [], []
    for kk in range(6):
        re, im = [], []
        for out, rows in ((re, slice(0, 8)), (im, slice(8, 16))):
            if 1 <= kk <= 4:
                out.append((total_a[rows, 0:128], kk - 1, 0))
            at = 128 + 32 * kk
            tile = at // 128
            out.append((total_a[rows, 128 * tile : 128 * tile + 128], (at % 128) // 32, 1))
        p_sum = jnp.zeros((8, 128), F32)
        q_sum = jnp.zeros((8, 128), F32)
        for value, source, kind in re:
            p_sum = p_sum + place(value, source, kind)
            q_sum = q_sum - place(value, source, kind + 2)
        for value, source, kind in im:
            p_sum = p_sum + place(value, source, kind + 2)
            q_sum = q_sum + place(value, source, kind)
        ps.append(p_sum)
        qs.append(q_sum)

    def row_transform(l, _):
        for b in range(4):
            out = jnp.zeros((8, 128), F32)
            for kk in range(6):
                at = 16 * b + 2 * kk
                out = out + twiddle[l, at] * ps[kk] + twiddle[l, at + 1] * qs[kk]
            part[4 * l + b] = out
        return 0

    lax.fori_loop(0, n_z, row_transform, 0)

    def four(z):
        return pl.ds(pl.multiple_of(4 * z, 4), 4)

    bz_copies = remote_to(
        [(part.at[four(l)], part_z.at[z], row_at(y, l, core), j) for l in levels], bz_send, bz_recv
    )
    begin(bz_copies)
    part_z[z] = part[four(z)]

    def forward(k):
        at = min(6 * k, 28)
        rows = pl.ds(at + 2, 8)
        pre = dot(band_one[1], lext[rows].reshape(256, 640), NN)
        pre = pre + dot(band_one[0], l_shift[0, rows].reshape(256, 640), NN)
        pre = pre + dot(band_one[2], l_shift[1, rows].reshape(256, 640), NN)
        square = pre * pre
        bend = jnp.tanh(pre * (GELU_A + (GELU_A * GELU_B) * square))
        half = 0.5 + 0.5 * bend
        hidden = (pre * half).astype(BF16)
        rise = half + pre * (0.5 - 0.5 * (bend * bend)) * (GELU_A + (3.0 * GELU_A * GELU_B) * square)
        slope[pl.ds(at, 6)] = rise[:, 0:512].reshape(6, 32, 512)
        to = pl.ds(at, 6)
        h_shift[1, to] = hidden[:, 0:512].reshape(6, 32, 512)
        h_shift[0, to] = shifted(hidden, 1)[:, 0:512].reshape(6, 32, 512)
        h_shift[2, to] = shifted(hidden, -1)[:, 0:512].reshape(6, 32, 512)

    for k in range(6):
        forward(k)
    arrive(bz_copies)
    value = part_z[0]
    for k in range(1, n_z):
        value = value + part_z[k]
    quad_sum[...] = value
    bq_copies = remote_to(
        [(quad_sum.at[2 * a + b], part_q.at[quarter], row_at(a, z, b), j) for a, b in quarters],
        bq_send, bq_recv,
    )
    begin(bq_copies)
    part_q[quarter] = quad_sum[quarter]
    sum_one[...] = jnp.zeros_like(sum_one)
    sum_two[...] = jnp.zeros_like(sum_two)
    counted = lax.broadcasted_iota(jnp.int32, (192, 512), 0) < 128

    def backward(k):
        at = min(6 * k, 26)
        rows = pl.ds(at + 3, 8)
        grad = dot(band_back[1], cext[rows, :, 0:512].reshape(256, 512), NN)
        grad = grad + dot(band_back[0], c_shift[1, rows].reshape(256, 512), NN)
        grad = grad + dot(band_back[2], c_shift[0, rows].reshape(256, 512), NN)
        pre_grad = grad * slope[pl.ds(at + 1, 6)].reshape(192, 512)
        if k == 5:
            pre_grad = jnp.where(counted, 0.0, pre_grad)
        pre_grad = pre_grad.astype(BF16)
        own = cext[pl.ds(at + 4, 6), :, 0:512].reshape(192, 512)
        if k == 5:
            own = jnp.where(counted, 0.0, own.astype(F32)).astype(BF16)
        for v in range(3):
            sum_two[v] += dot(own, h_shift[v, pl.ds(at, 8)].reshape(256, 512), NT)
            if v == 1:
                layer = lext[rows, :, 0:512]
            else:
                layer = l_shift[v // 2, rows, :, 0:512]
            sum_one[v] += dot(pre_grad, layer.reshape(256, 512), NT)

    for k in range(2):
        backward(k)
    arrive(bq_copies)
    spectrum = part_q[0] + part_q[1] + part_q[2] + part_q[3]

    groups = lane_group((8, 128))
    row = lax.broadcasted_iota(jnp.int32, (8, 128), 0)
    first = (row == 0) & (j % 4 == 0)
    twice = jnp.where(first, 1.0, 2.0)
    spectrum = spectrum * jnp.where(groups % 2 == 1, twice * scaling, scaling)
    s_re = everywhere(jnp.where(groups == 0, spectrum, 0.0))
    m_re = everywhere(jnp.where(groups == 1, spectrum, 0.0))
    s_im = everywhere(jnp.where(groups == 2, spectrum, 0.0))
    m_im = everywhere(jnp.where(groups == 3, spectrum, 0.0))
    wide = lane_group((16, 256)) == lax.broadcasted_iota(jnp.int32, (16, 256), 0) % 8
    both = jnp.concatenate([s_re, s_im], axis=0)[:, 0:32]
    both = jnp.concatenate(parts_of(both, 3), axis=0)
    by = dot(both, jnp.concatenate([w_real[...].reshape(256, 32), w_imag[...].reshape(256, 32)], axis=0), NT)
    by = by[0:16] + by[16:32] + by[32:48]
    by_real = jnp.where(wide, by[:, 0:256], 0.0)
    by_imag = jnp.where(wide, by[:, 256:512], 0.0)
    mixed_re = by_real[0:8] - by_imag[8:16]
    mixed_im = by_real[8:16] + by_imag[0:8]
    mixed_re = everywhere(mixed_re[:, 0:128] + mixed_re[:, 128:256])
    mixed_im = everywhere(mixed_im[:, 0:128] + mixed_im[:, 128:256])
    quad[quarter] = jnp.where(
        groups == 1, mixed_im, jnp.where(groups == 2, -mixed_im, mixed_re)
    )

    cq_copies = remote_to(
        [(quad.at[quarter], quad.at[quarter], row_at(a, z, b), j) for a, b in quarters], cq_send, cq_recv
    )
    begin(cq_copies)
    grads = jnp.concatenate(
        [jnp.concatenate([m_re, m_re], axis=1), jnp.concatenate([m_im, m_im], axis=1)], axis=0
    )
    grads = jnp.where(wide, grads, 0.0)
    fields = jnp.concatenate(
        [jnp.where(groups == 0, s_re, -s_im), jnp.where(groups == 0, s_im, s_re)], axis=0
    )
    outer = dot(grads, fields, TN, HIGH)
    outer_out[...] = outer

    for k in range(2, 4):
        backward(k)
    arrive(cq_copies)
    cz_copies = remote_to(
        [(quad, mixed_in.at[four(z)], row_at(y, l, core), j) for l in levels], cz_send, cz_recv
    )
    begin(cz_copies)
    mixed_in[four(z)] = quad[...]
    for k in range(4, 6):
        backward(k)

    for n, sums in enumerate((sum_one, sum_two)):
        for v in range(3):
            total = jnp.zeros((32, 256), F32)
            for r in range(6):
                value = sums[v, 32 * r : 32 * r + 32, :]
                total = total + (pltpu.roll(value, 256 - 32 * r, 1) if r else value)
            for e in range(4):
                at = 12 * n + 4 * v + e
                mine[at // 3, 8 * (at % 3) : 8 * (at % 3) + 8, :] = total[8 * e : 8 * e + 8, 0:128]

    r_copies = remote_to([(mine.at[c], sum_c.at[j], i, c) for c in cols], r_send, r_recv)
    begin(r_copies)
    sum_c[j] = mine[j]

    arrive(cz_copies)
    def inverse(l, sums):
        sums = list(sums)
        for b in range(4):
            value = mixed_in[4 * l + b]
            for n in range(12):
                sums[n] = sums[n] + twiddle[l, 16 * b + n] * value
        return tuple(sums)

    zero = jnp.zeros((8, 128), F32)
    sums = lax.fori_loop(0, n_z, inverse, (zero,) * 12)
    grown = twice * scaling
    tiles = [zero] * 4
    for kk in range(6):
        value = (sums[2 * kk] + pltpu.roll(sums[2 * kk + 1], 64, 1)) * grown
        tiles[kk // 4] = tiles[kk // 4] + place(value, 0, kk % 4)
        tiles[2 + kk // 4] = tiles[2 + kk // 4] + place(value, 1, kk % 4)
    folded[0:8, 0:128] = tiles[0]
    folded[0:8, 128:256] = tiles[1]
    folded[8:16, 0:128] = tiles[2]
    folded[8:16, 128:256] = tiles[3]

    d_copies = remote_to([(folded, folded_in.at[j], i, c) for c in cols], d_send, d_recv)
    begin(d_copies)
    folded_in[j] = folded[...]

    arrive(r_copies)
    value = sum_c[0]
    for k in range(1, n_col):
        value = value + sum_c[k]
    chunk_c[...] = value
    rq_copies = remote_to(
        [(chunk_c, sum_q.at[quarter], row_at(a, z, b), j) for a, b in quarters], rq_send, rq_recv
    )
    begin(rq_copies)
    sum_q[quarter] = value

    arrive(rq_copies)
    value = sum_q[0] + sum_q[1] + sum_q[2] + sum_q[3]
    chunk_q[...] = value
    rz_copies = remote_to(
        [(chunk_q, sum_z.at[z], row_at(y, l, core), j) for l in levels], rz_send, rz_recv
    )
    begin(rz_copies)
    sum_z[z] = value

    arrive(d_copies)
    waves = (folded_in[0:4] + folded_in[4:8]).reshape(64, 256)
    upper, lower = parts_of(waves, 2)
    smooth = dot(
        jnp.concatenate([upper, upper, lower], axis=0),
        jnp.concatenate([tab[1], tab[1, 0:64]], axis=0),
        TN,
    )[0:192]
    upper = smooth.astype(BF16)
    high[...] = upper
    low[...] = (smooth - upper.astype(F32)).astype(BF16)

    def window(t):
        coarse = slice(32 * t, 32 * t + 96)
        rest = [h_shift[v, 8 * t + 8 : 8 * t + 10].reshape(64, 512) for v in range(3)]
        rest = jnp.concatenate(rest + [high[coarse, :], low[coarse, :]], axis=0)
        total = dot(band_tail[...], rest, NN)
        for v in range(3):
            total = total + dot(band_two[v], h_shift[v, 8 * t : 8 * t + 8].reshape(256, 512), NN)
        return total.reshape(32, 8, 512)

    results = []
    for t in range(2):
        rows = slice(16 * t, 16 * t + 16)
        value = jnp.concatenate([window(2 * t), window(2 * t + 1)], axis=1)
        stage[:, rows, :] = value.astype(BF16)
        results.append(
            pltpu.make_async_copy(stage.at[:, rows], stage_out.at[:, rows], local_sem.at[14 + t])
        )
        results[t].start()

    arrive(rz_copies)
    value = sum_z[0]
    for k in range(1, n_z):
        value = value + sum_z[k]
    value = value * scale
    done[...] = value
    g_copies = remote_to([(done, gathered.at[j], i, c) for c in cols], g_send, g_recv)
    begin(g_copies)
    gathered[j] = value
    for copies in (
        a_copies, halos, bz_copies, bq_copies, cq_copies, cz_copies, r_copies, d_copies, rq_copies, rz_copies
    ):
        leave(copies)
    arrive(g_copies)
    total_out[...] = gathered[...]
    leave(g_copies)
    for copy in results:
        copy.wait()


def finish_kernel(stage, total, outer, out, out_one, out_two, g_real, g_imag, held, sem):
    pieces = [slice(8 * n, 8 * n + 8) for n in range(4)]
    inward = [pltpu.make_async_copy(stage.at[p], held.at[p], sem.at[n]) for n, p in enumerate(pieces)]
    outward = [pltpu.make_async_copy(held.at[p], out.at[p], sem.at[4 + n]) for n, p in enumerate(pieces)]
    begin(inward)
    for n in range(4):
        inward[n].wait()
        outward[n].start()
    value = total[...].reshape(192, 128)
    for n, grad in enumerate((out_one, out_two)):
        for v in range(3):
            at = 96 * n + 32 * v
            for u in range(3):
                grad[3 * u + v] = value[at : at + 32, 32 * u : 32 * u + 32]
    g_real[...] = outer[:, 0:32].reshape(8, 32, 32)
    g_imag[...] = outer[:, 32:64].reshape(8, 32, 32)
    for copy in outward:
        copy.wait()


def body(n_row, n_col, features, mask, mask_gain, conv_one, conv_two, spec_real, spec_imag, cotangent):
    total_rows, total_cols = 32 * n_row, 512 * n_col
    scaling = 1.0 / math.sqrt((total_rows // RATIO) * (total_cols // RATIO))
    vmem = pl.BlockSpec(memory_space=pltpu.VMEM)
    hbm = pl.BlockSpec(memory_space=pl.ANY)
    col_tab = jnp.asarray(column_tables(n_col))
    row_tab = jnp.asarray(row_tables(n_row))
    spread = jnp.asarray(expand_table(), BF16)
    stretch = jnp.asarray(prolong_table(), BF16)
    turn = jnp.asarray(turn_table(), BF16)
    n_z = n_row // 4
    dma = pltpu.SemaphoreType.DMA
    stage, total, outer = pl.pallas_call(
        functools.partial(
            main_kernel, n_row, n_col, scaling, 1.0 / math.sqrt(total_rows * total_cols)
        ),
        out_shape=[
            jax.ShapeDtypeStruct((32, 32, 512), BF16),
            jax.ShapeDtypeStruct((n_col, 24, 128), F32),
            jax.ShapeDtypeStruct((256, 128), F32),
        ],
        in_specs=[hbm] * 2 + [pl.BlockSpec(memory_space=pltpu.SMEM)] + [hbm] * 10,
        out_specs=[hbm, vmem, vmem],
        scratch_shapes=[
            pltpu.VMEM((32, 32, 512), BF16),
            pltpu.VMEM((32, 512), jnp.int32),
            pltpu.VMEM((32, 32, 512), BF16),
            pltpu.VMEM((8, 32, 32), BF16),
            pltpu.VMEM((8, 32, 32), BF16),
            pltpu.VMEM((9, 32, 32), BF16),
            pltpu.VMEM((9, 32, 32), BF16),
            pltpu.VMEM(spread.shape, BF16),
            pltpu.VMEM(stretch.shape, BF16),
            pltpu.VMEM(turn.shape, BF16),
            pltpu.VMEM((32, 32, 512), BF16),
            pltpu.VMEM((40, 32, 640), BF16),
            pltpu.VMEM((40, 32, 640), BF16),
            pltpu.VMEM((192, 512), BF16),
            pltpu.VMEM((192, 512), BF16),
            pltpu.VMEM((10, 32, 512), F32),
            pltpu.VMEM((2, 128, 512), BF16),
            pltpu.SMEM(row_tab.shape[1:], F32),
            pltpu.VMEM((64, 384), F32),
            pltpu.VMEM((n_col, 16, 384), F32),
            pltpu.VMEM((n_row, 8, 128), F32),
            pltpu.VMEM((n_z, 4, 8, 128), F32),
            pltpu.VMEM((4, 8, 128), F32),
            pltpu.VMEM((4, 8, 128), F32),
            pltpu.VMEM((4, 8, 128), F32),
            pltpu.VMEM((n_row, 8, 128), F32),
            pltpu.VMEM((16, 256), F32),
            pltpu.VMEM((n_col, 16, 256), F32),
            pltpu.VMEM((4, 1024), F32),
            pltpu.VMEM((4, 1024), F32),
            pltpu.VMEM((2, 4, 1280), F32),
            pltpu.VMEM((2, 2, 32, 512), BF16),
            pltpu.VMEM((2, 1, 32, 512), BF16),
            pltpu.VMEM((2, 40, 32, 640), BF16),
            pltpu.VMEM((2, 40, 32, 512), BF16),
            pltpu.VMEM((3, 34, 32, 512), BF16),
            pltpu.VMEM((34, 32, 512), F32),
            pltpu.VMEM((3, 192, 256), BF16),
            pltpu.VMEM((3, 256, 256), BF16),
            pltpu.VMEM((256, 384), BF16),
            pltpu.VMEM((3, 192, 256), BF16),
            pltpu.VMEM((3, 192, 256), F32),
            pltpu.VMEM((3, 192, 256), F32),
            pltpu.VMEM((n_col, 24, 128), F32),
            pltpu.VMEM((n_col, 24, 128), F32),
            pltpu.VMEM((24, 128), F32),
            pltpu.VMEM((4, 24, 128), F32),
            pltpu.VMEM((24, 128), F32),
            pltpu.VMEM((n_z, 24, 128), F32),
            pltpu.VMEM((24, 128), F32),
            pltpu.VMEM((n_col, 24, 128), F32),
            dma((16,)),
            dma((10,)),
            dma((10,)),
            *[dma((7,))] * 20,
        ],
        compiler_params=pltpu.CompilerParams(
            collective_id=0, has_side_effects=True, vmem_limit_bytes=VMEM_LIMIT
        ),
        name="layer",
    )(
        features, mask, mask_gain, cotangent, spec_real, spec_imag, conv_one, conv_two,
        spread, stretch, turn, col_tab, row_tab,
    )
    return pl.pallas_call(
        finish_kernel,
        out_shape=[
            jax.ShapeDtypeStruct((32, 32, 512), BF16),
            jax.ShapeDtypeStruct((9, 32, 32), F32),
            jax.ShapeDtypeStruct((9, 32, 32), F32),
            jax.ShapeDtypeStruct((8, 32, 32), F32),
            jax.ShapeDtypeStruct((8, 32, 32), F32),
        ],
        in_specs=[hbm, vmem, vmem],
        out_specs=[hbm] + [vmem] * 4,
        scratch_shapes=[pltpu.VMEM((32, 32, 512), BF16), dma((8,))],
        compiler_params=pltpu.CompilerParams(vmem_limit_bytes=VMEM_LIMIT),
        name="finish",
    )(stage, total, outer)


def solution(mesh):
    n_row, n_col = mesh.shape["row"], mesh.shape["col"]
    placed = (
        P(None, "row", "col"),
        P("row", "col"),
        P(),
        P(),
        P(),
        P(("row", "col"), None, None),
        P(("row", "col"), None, None),
        P(None, "row", "col"),
    )
    return jax.shard_map(
        functools.partial(body, n_row, n_col),
        mesh=mesh,
        in_specs=placed,
        out_specs=(
            P(None, "row", "col"),
            P(),
            P(),
            P(("row", "col"), None, None),
            P(("row", "col"), None, None),
        ),
        check_vma=False,
    )
```

profile of v0, /device:TPU:1, one launch (start us, length us, event | category | flops | bytes accessed | tf_op | source)
XLA Modules:
  0.0 59.2 jit_solution(15894974685649571354)
XLA Ops:
  0.6 54.7 %layer.1 = (bf16[32,32,512]{2,1,0:T(8,128)(2,1)}, f32[8,24,128]{2,1,0:T(8,128)}, f32[256,128]{1,0:T(8,128)}) custom-call(bf16[32,32,512]{2,1,0:T(8,128)(2,1)} %feat_h.1, s32[32,512]{1,0:T(8,128)} %mask_h.1, f32[32]{0:T(128)} %gain.1, bf16[32,32,512]{2,1,0:T(8,128)(2,1)} %cot_h.1, bf16[8,32,32]{2,1,0:T(8,128)(2,1)} %real_h.1, bf16[8,32,32]{2,1,0:T(8,128)(2,1)} %imag_h.1, ...), custom_call_target="tpu_custom_call" | custom-call | tf_op jit(solution)/shard_map/layer/pallas_call | solution.py:676
  55.3 3.7 %finish.1 = (bf16[32,32,512]{2,1,0:T(8,128)(2,1)}, f32[9,32,32]{2,1,0:T(8,128)}, f32[9,32,32]{2,1,0:T(8,128)}, f32[8,32,32]{2,1,0:T(8,128)}, f32[8,32,32]{2,1,0:T(8,128)}) custom-call(bf16[32,32,512]{2,1,0:T(8,128)(2,1)} %get-tuple-element.8.stage, f32[8,24,128]{2,1,0:T(8,128)} %get-tuple-element.9.total, f32[256,128]{1,0:T(8,128)} %get-tuple-element.10.outer), custom_call_target="tpu_custom_call" | custom-call | tf_op jit(solution)/shard_map/finish/pallas_call | solution.py:752
where the time goes:
time: 59.4 us; the launch traced here: 59.2 us
  Pallas kernels  58.4 us (98%)
  between operations  0.8 us (1%)
    pallas_call x1, Pallas kernels, body(): pl.pallas_call(functools.partial(main_kernel, n_row, n_col, scaling, 1.0...  54.7 us
    pallas_call x1, Pallas kernels, body(): pl.pallas_call(finish_kernel, out_shape=[jax.ShapeDtypeStruct((32, 32, 51...  3.73 us

commit v1 on v0

--- a/solution.py
+++ b/solution.py
@@ -58,21 +58,24 @@
 
 
 def row_tables(n_row):
-    n_z = n_row // 4
-    peers = np.arange(n_row).reshape(2, n_z, 2).transpose(1, 0, 2).reshape(-1)
     n_one = 4 * n_row
     q_all = np.arange(2 * n_row)
     f1 = np.where(q_all < n_row, q_all, n_one - 2 * n_row + q_all)
-    out = np.zeros((2 * n_row, n_row, 16))
+
+    def waves(q, rows):
+        phase = 2 * np.pi * ((f1[q][:, None] * rows[None, :]) % n_one) / n_one
+        return np.stack([np.cos(phase), np.sin(phase)], axis=-1).reshape(len(q), -1)
+
+    there, back = [], []
     for i in range(n_row):
         for h in range(2):
-            q = 2 * peers + h
-            for kk in range(6):
-                phase = 2 * np.pi * ((f1[q] * (4 * i + kk - 1)) % n_one) / n_one
-                out[2 * i + h, :, 2 * kk] = np.cos(phase)
-                out[2 * i + h, :, 2 * kk + 1] = np.sin(phase)
-    out = out.reshape(2 * n_row, n_z, 64)
-    return np.pad(out, ((0, 0), (0, 0), (0, 64))).astype(np.float32)
+            peers = 2 * np.arange(n_row // 2) + i % 2
+            value = waves(2 * peers + h, 8 * (i // 2) - 1 + np.arange(10))
+            there.append(np.pad(value, ((0, 0), (0, 12))).reshape(-1, 128))
+            value = waves(2 * np.arange(n_row) + h, 4 * i - 1 + np.arange(6))
+            value = np.pad(value, ((0, 0), (0, 4))).reshape(-1, 64)
+            back.append(np.pad(value, ((0, 0), (0, 64))))
+    return np.stack(there).astype(np.float32), np.stack(back).astype(np.float32)
 
 
 def prolong_table():
@@ -208,32 +211,33 @@
 
 def main_kernel(
     n_row, n_col, scaling, scale,
-    feat_h, mask_h, gain, cot_h, real_h, imag_h, one_h, two_h, spread_h, stretch_h, turn_h, col_tab, row_tab,
+    feat_h, mask_h, gain, cot_h, real_h, imag_h, one_h, two_h, spread_h, stretch_h, turn_h, col_tab, row_tab, back_tab,
     stage_out, total_out, outer_out,
     feat, mask, cot, w_real, w_imag, w_one, w_two, spread, stretch, turn, stage,
-    lext, cext, high, low, field, tab, twiddle,
-    share, share_in, part, part_z, quad_sum, part_q, quad, mixed_in, folded, folded_in,
+    lext, cext, high, low, field, tab, twiddle, twiddle_back,
+    share, share_in, pair_in, part, part_in, duo, mixed_in, folded, folded_in,
     left, right, side_in, rows_in, row_c_in,
     l_shift, c_shift, h_shift, slope, band_one, band_two, band_tail, band_back, sum_one, sum_two,
-    mine, sum_c, chunk_c, sum_q, chunk_q, sum_z, done, gathered,
-    local_sem, halo_send, halo_recv, a_send, a_recv, bz_send, bz_recv, bq_send, bq_recv,
-    cq_send, cq_recv, cz_send, cz_recv, d_send, d_recv,
-    r_send, r_recv, rq_send, rq_recv, rz_send, rz_recv, g_send, g_recv,
+    mine, half_in, mine_half, sum_c, chunk, sum_g, done, gathered,
+    local_sem, halo_send, halo_recv, a_send, a_recv, zp_send, zp_recv, b_send, b_recv, cp_send, cp_recv,
+    c_send, c_recv, d_send, d_recv, rp_send, rp_recv, r_send, r_recv, rg_send, rg_recv, g_send, g_recv,
+    gp_send, gp_recv,
 ):
     i = lax.axis_index("row")
     j = lax.axis_index("col")
     half = j // 4
-    n_z = n_row // 4
-    y, z, core = i // (2 * n_z), (i // 2) % n_z, i % 2
-    quarter = 2 * y + core
+    core = i % 2
+    other = 1 - core
+    pair = i + 1 - 2 * core
+    n_chip = n_row // 2
+    chip = i // 2
     up, down = (i + n_row - 1) % n_row, (i + 1) % n_row
     west, east = (j + n_col - 1) % n_col, (j + 1) % n_col
     cols = [(j + d) % n_col for d in range(1, n_col)]
-    levels = [(z + d) % n_z for d in range(1, n_z)]
-    quarters = [(y, 1 - core), (1 - y, core), (1 - y, 1 - core)]
-
-    def row_at(y, z, core):
-        return (y * n_z + z) * 2 + core
+    chips = [(chip + d) % n_chip for d in range(1, n_chip)]
+
+    def here(chip):
+        return 2 * chip + core
 
     loads = [
         pltpu.make_async_copy(src, dst, local_sem.at[n])
@@ -247,6 +251,7 @@
                 (cot_h.at[:, 16:32], cot.at[:, 16:32]),
                 (col_tab.at[j], tab),
                 (row_tab.at[2 * i + half], twiddle),
+                (back_tab.at[2 * i + half], twiddle_back),
                 (one_h, w_one),
                 (two_h, w_two),
                 (spread_h, spread),
@@ -261,8 +266,8 @@
     barrier = pltpu.get_barrier_semaphore()
     partners = (
         [(i, c) for c in cols]
-        + [(row_at(y, l, core), j) for l in levels]
-        + [(row_at(a, z, b), j) for a, b in quarters]
+        + [(here(g), j) for g in chips]
+        + [(pair, j)]
         + [(r, c) for r in (up, down) for c in (j, west, east)]
     )
     for partner in partners:
@@ -354,6 +359,13 @@
     band_tail[:, 192:288] = stretch[...]
     band_tail[:, 288:384] = stretch[...]
 
+    arrive(a_copies)
+    total_a = share_in[0]
+    for k in range(1, n_col):
+        total_a = total_a + share_in[k]
+    pair_in[core] = total_a
+    zp_copies = remote_to([(pair_in.at[core], pair_in.at[core], pair, j)], zp_send, zp_recv)
+    begin(zp_copies)
     arrive(halos)
     lext[2:4, :, 0:512] = rows_in[0]
     lext[36:38, :, 0:512] = rows_in[1]
@@ -377,49 +389,40 @@
     for k in range(9):
         move(k)
 
-    arrive(a_copies)
-    total_a = share_in[0]
-    for k in range(1, n_col):
-        total_a = total_a + share_in[k]
+    arrive(zp_copies)
     ps, qs = [], []
-    for kk in range(6):
-        re, im = [], []
-        for out, rows in ((re, slice(0, 8)), (im, slice(8, 16))):
-            if 1 <= kk <= 4:
-                out.append((total_a[rows, 0:128], kk - 1, 0))
-            at = 128 + 32 * kk
-            tile = at // 128
-            out.append((total_a[rows, 128 * tile : 128 * tile + 128], (at % 128) // 32, 1))
+    for n in range(10):
         p_sum = jnp.zeros((8, 128), F32)
         q_sum = jnp.zeros((8, 128), F32)
-        for value, source, kind in re:
-            p_sum = p_sum + place(value, source, kind)
-            q_sum = q_sum - place(value, source, kind + 2)
-        for value, source, kind in im:
-            p_sum = p_sum + place(value, source, kind + 2)
-            q_sum = q_sum + place(value, source, kind)
+        for b in range(2):
+            kk = n - 4 * b
+            if not 0 <= kk <= 5:
+                continue
+            pieces = [(128 + 32 * kk, 1)]
+            if 1 <= kk <= 4:
+                pieces.append((32 * kk - 32, 0))
+            for at, kind in pieces:
+                lanes = slice(128 * (at // 128), 128 * (at // 128) + 128)
+                re, im = pair_in[b, 0:8, lanes], pair_in[b, 8:16, lanes]
+                source = (at % 128) // 32
+                p_sum = p_sum + place(re, source, kind) + place(im, source, kind + 2)
+                q_sum = q_sum + place(im, source, kind) - place(re, source, kind + 2)
         ps.append(p_sum)
         qs.append(q_sum)
 
     def row_transform(l, _):
         for b in range(4):
             out = jnp.zeros((8, 128), F32)
-            for kk in range(6):
-                at = 16 * b + 2 * kk
-                out = out + twiddle[l, at] * ps[kk] + twiddle[l, at + 1] * qs[kk]
+            for n in range(10):
+                at = 32 * b + 2 * n
+                out = out + twiddle[l, at] * ps[n] + twiddle[l, at + 1] * qs[n]
             part[4 * l + b] = out
         return 0
 
-    lax.fori_loop(0, n_z, row_transform, 0)
-
-    def four(z):
-        return pl.ds(pl.multiple_of(4 * z, 4), 4)
-
-    bz_copies = remote_to(
-        [(part.at[four(l)], part_z.at[z], row_at(y, l, core), j) for l in levels], bz_send, bz_recv
-    )
-    begin(bz_copies)
-    part_z[z] = part[four(z)]
+    lax.fori_loop(0, n_chip // 4, row_transform, 0)
+    b_copies = remote_to([(part.at[g], part_in.at[chip], here(g), j) for g in chips], b_send, b_recv)
+    begin(b_copies)
+    part_in[chip] = part[chip]
 
     def forward(k):
         at = min(6 * k, 28)
@@ -440,17 +443,6 @@
 
     for k in range(6):
         forward(k)
-    arrive(bz_copies)
-    value = part_z[0]
-    for k in range(1, n_z):
-        value = value + part_z[k]
-    quad_sum[...] = value
-    bq_copies = remote_to(
-        [(quad_sum.at[2 * a + b], part_q.at[quarter], row_at(a, z, b), j) for a, b in quarters],
-        bq_send, bq_recv,
-    )
-    begin(bq_copies)
-    part_q[quarter] = quad_sum[quarter]
     sum_one[...] = jnp.zeros_like(sum_one)
     sum_two[...] = jnp.zeros_like(sum_two)
     counted = lax.broadcasted_iota(jnp.int32, (192, 512), 0) < 128
@@ -476,10 +468,30 @@
                 layer = l_shift[v // 2, rows, :, 0:512]
             sum_one[v] += dot(pre_grad, layer.reshape(256, 512), NT)
 
-    for k in range(2):
+    for k in range(6):
         backward(k)
-    arrive(bq_copies)
-    spectrum = part_q[0] + part_q[1] + part_q[2] + part_q[3]
+    for n, sums in enumerate((sum_one, sum_two)):
+        for v in range(3):
+            total = jnp.zeros((32, 256), F32)
+            for r in range(6):
+                value = sums[v, 32 * r : 32 * r + 32, :]
+                total = total + (pltpu.roll(value, 256 - 32 * r, 1) if r else value)
+            for e in range(8):
+                at = 96 * n + 32 * v + 4 * e
+                piece = at // 12
+                mine[piece // n_col, piece % n_col, at % 12 : at % 12 + 4, :] = total[4 * e : 4 * e + 4, 0:128]
+    rp_copies = remote_to([(mine.at[other], half_in, pair, j)], rp_send, rp_recv)
+    begin(rp_copies)
+    arrive(rp_copies)
+    mine_half[...] = mine[core] + half_in[...]
+    r_copies = remote_to([(mine_half.at[c], sum_c.at[j], i, c) for c in cols], r_send, r_recv)
+    begin(r_copies)
+    sum_c[j] = mine_half[j]
+
+    arrive(b_copies)
+    spectrum = part_in[0]
+    for k in range(1, n_chip):
+        spectrum = spectrum + part_in[k]
 
     groups = lane_group((8, 128))
     row = lax.broadcasted_iota(jnp.int32, (8, 128), 0)
@@ -501,14 +513,19 @@
     mixed_im = by_real[8:16] + by_imag[0:8]
     mixed_re = everywhere(mixed_re[:, 0:128] + mixed_re[:, 128:256])
     mixed_im = everywhere(mixed_im[:, 0:128] + mixed_im[:, 128:256])
-    quad[quarter] = jnp.where(
-        groups == 1, mixed_im, jnp.where(groups == 2, -mixed_im, mixed_re)
-    )
-
-    cq_copies = remote_to(
-        [(quad.at[quarter], quad.at[quarter], row_at(a, z, b), j) for a, b in quarters], cq_send, cq_recv
-    )
-    begin(cq_copies)
+    upper = jnp.where(groups == 0, mixed_re, mixed_im)
+    duo[core] = jnp.where(groups[0:4] < 2, upper[0:4], jnp.where(groups[0:4] == 2, mixed_re[4:8], mixed_im[4:8]))
+
+    cp_copies = remote_to([(duo.at[core], duo.at[core], pair, j)], cp_send, cp_recv)
+    begin(cp_copies)
+    arrive(cp_copies)
+
+    def two(chip):
+        return pl.ds(pl.multiple_of(2 * chip, 2), 2)
+
+    c_copies = remote_to([(duo, mixed_in.at[two(chip)], here(g), j) for g in chips], c_send, c_recv)
+    begin(c_copies)
+    mixed_in[two(chip)] = duo[...]
     grads = jnp.concatenate(
         [jnp.concatenate([m_re, m_re], axis=1), jnp.concatenate([m_im, m_im], axis=1)], axis=0
     )
@@ -519,77 +536,49 @@
     outer = dot(grads, fields, TN, HIGH)
     outer_out[...] = outer
 
-    for k in range(2, 4):
-        backward(k)
-    arrive(cq_copies)
-    cz_copies = remote_to(
-        [(quad, mixed_in.at[four(z)], row_at(y, l, core), j) for l in levels], cz_send, cz_recv
-    )
-    begin(cz_copies)
-    mixed_in[four(z)] = quad[...]
-    for k in range(4, 6):
-        backward(k)
-
-    for n, sums in enumerate((sum_one, sum_two)):
-        for v in range(3):
-            total = jnp.zeros((32, 256), F32)
-            for r in range(6):
-                value = sums[v, 32 * r : 32 * r + 32, :]
-                total = total + (pltpu.roll(value, 256 - 32 * r, 1) if r else value)
-            for e in range(4):
-                at = 12 * n + 4 * v + e
-                mine[at // 3, 8 * (at % 3) : 8 * (at % 3) + 8, :] = total[8 * e : 8 * e + 8, 0:128]
-
-    r_copies = remote_to([(mine.at[c], sum_c.at[j], i, c) for c in cols], r_send, r_recv)
-    begin(r_copies)
-    sum_c[j] = mine[j]
-
-    arrive(cz_copies)
+    arrive(r_copies)
+    value = sum_c[0]
+    for k in range(1, n_col):
+        value = value + sum_c[k]
+    chunk[...] = value
+    rg_copies = remote_to([(chunk, sum_g.at[chip], here(g), j) for g in chips], rg_send, rg_recv)
+    begin(rg_copies)
+    sum_g[chip] = value
+
+    arrive(c_copies)
     def inverse(l, sums):
         sums = list(sums)
         for b in range(4):
             value = mixed_in[4 * l + b]
             for n in range(12):
-                sums[n] = sums[n] + twiddle[l, 16 * b + n] * value
+                sums[n] = sums[n] + twiddle_back[l, 16 * b + n] * value
         return tuple(sums)
 
-    zero = jnp.zeros((8, 128), F32)
-    sums = lax.fori_loop(0, n_z, inverse, (zero,) * 12)
-    grown = twice * scaling
-    tiles = [zero] * 4
+    sums = lax.fori_loop(0, n_row // 4, inverse, (jnp.zeros((4, 128), F32),) * 12)
+    folded[:, 192:256] = jnp.zeros((16, 64), F32)
+    grown = jnp.where((groups[0:4] < 2), twice[0:4], 2.0) * scaling
+    even = groups[0:4] % 2 == 0
     for kk in range(6):
-        value = (sums[2 * kk] + pltpu.roll(sums[2 * kk + 1], 64, 1)) * grown
-        tiles[kk // 4] = tiles[kk // 4] + place(value, 0, kk % 4)
-        tiles[2 + kk // 4] = tiles[2 + kk // 4] + place(value, 1, kk % 4)
-    folded[0:8, 0:128] = tiles[0]
-    folded[0:8, 128:256] = tiles[1]
-    folded[8:16, 0:128] = tiles[2]
-    folded[8:16, 128:256] = tiles[3]
+        sines = sums[2 * kk + 1]
+        sines = jnp.where(even, -pltpu.roll(sines, 96, 1), pltpu.roll(sines, 32, 1))
+        value = (sums[2 * kk] + sines) * grown
+        for n in range(4):
+            at = 8 * (n % 2) + 4 * (n // 2)
+            folded[at : at + 4, 32 * kk : 32 * kk + 32] = value[:, 32 * n : 32 * n + 32]
 
     d_copies = remote_to([(folded, folded_in.at[j], i, c) for c in cols], d_send, d_recv)
     begin(d_copies)
     folded_in[j] = folded[...]
 
-    arrive(r_copies)
-    value = sum_c[0]
-    for k in range(1, n_col):
-        value = value + sum_c[k]
-    chunk_c[...] = value
-    rq_copies = remote_to(
-        [(chunk_c, sum_q.at[quarter], row_at(a, z, b), j) for a, b in quarters], rq_send, rq_recv
-    )
-    begin(rq_copies)
-    sum_q[quarter] = value
-
-    arrive(rq_copies)
-    value = sum_q[0] + sum_q[1] + sum_q[2] + sum_q[3]
-    chunk_q[...] = value
-    rz_copies = remote_to(
-        [(chunk_q, sum_z.at[z], row_at(y, l, core), j) for l in levels], rz_send, rz_recv
-    )
-    begin(rz_copies)
-    sum_z[z] = value
-
+    arrive(rg_copies)
+    value = sum_g[0]
+    for k in range(1, n_chip):
+        value = value + sum_g[k]
+    value = value * scale
+    done[...] = value
+    g_copies = remote_to([(done, gathered.at[core, j], i, c) for c in cols], g_send, g_recv)
+    begin(g_copies)
+    gathered[core, j] = value
     arrive(d_copies)
     waves = (folded_in[0:4] + folded_in[4:8]).reshape(64, 256)
     upper, lower = parts_of(waves, 2)
@@ -617,39 +606,30 @@
         value = jnp.concatenate([window(2 * t), window(2 * t + 1)], axis=1)
         stage[:, rows, :] = value.astype(BF16)
         results.append(
-            pltpu.make_async_copy(stage.at[:, rows], stage_out.at[:, rows], local_sem.at[14 + t])
+            pltpu.make_async_copy(stage.at[:, rows], stage_out.at[:, rows], local_sem.at[15 + t])
         )
         results[t].start()
 
-    arrive(rz_copies)
-    value = sum_z[0]
-    for k in range(1, n_z):
-        value = value + sum_z[k]
-    value = value * scale
-    done[...] = value
-    g_copies = remote_to([(done, gathered.at[j], i, c) for c in cols], g_send, g_recv)
-    begin(g_copies)
-    gathered[j] = value
     for copies in (
-        a_copies, halos, bz_copies, bq_copies, cq_copies, cz_copies, r_copies, d_copies, rq_copies, rz_copies
+        a_copies, halos, zp_copies, b_copies, cp_copies, c_copies, d_copies, rp_copies, r_copies, rg_copies
     ):
         leave(copies)
     arrive(g_copies)
-    total_out[...] = gathered[...]
+    gp_copies = remote_to([(gathered.at[core], gathered.at[core], pair, j)], gp_send, gp_recv)
+    begin(gp_copies)
     leave(g_copies)
     for copy in results:
         copy.wait()
-
-
-def finish_kernel(stage, total, outer, out, out_one, out_two, g_real, g_imag, held, sem):
-    pieces = [slice(8 * n, 8 * n + 8) for n in range(4)]
-    inward = [pltpu.make_async_copy(stage.at[p], held.at[p], sem.at[n]) for n, p in enumerate(pieces)]
-    outward = [pltpu.make_async_copy(held.at[p], out.at[p], sem.at[4 + n]) for n, p in enumerate(pieces)]
-    begin(inward)
-    for n in range(4):
-        inward[n].wait()
-        outward[n].start()
-    value = total[...].reshape(192, 128)
+    arrive(gp_copies)
+    for e in range(48):
+        piece, at = divmod(4 * e, 12)
+        total_out[4 * e : 4 * e + 4, :] = gathered[piece // n_col, piece % n_col, at : at + 4, :]
+    leave(gp_copies)
+
+
+def finish_kernel(stage, total, outer, out, out_one, out_two, g_real, g_imag):
+    out[...] = stage[...]
+    value = total[...]
     for n, grad in enumerate((out_one, out_two)):
         for v in range(3):
             at = 96 * n + 32 * v
@@ -657,8 +637,6 @@
                 grad[3 * u + v] = value[at : at + 32, 32 * u : 32 * u + 32]
     g_real[...] = outer[:, 0:32].reshape(8, 32, 32)
     g_imag[...] = outer[:, 32:64].reshape(8, 32, 32)
-    for copy in outward:
-        copy.wait()
 
 
 def body(n_row, n_col, features, mask, mask_gain, conv_one, conv_two, spec_real, spec_imag, cotangent):
@@ -667,11 +645,10 @@
     vmem = pl.BlockSpec(memory_space=pltpu.VMEM)
     hbm = pl.BlockSpec(memory_space=pl.ANY)
     col_tab = jnp.asarray(column_tables(n_col))
-    row_tab = jnp.asarray(row_tables(n_row))
+    row_tab, back_tab = (jnp.asarray(table) for table in row_tables(n_row))
     spread = jnp.asarray(expand_table(), BF16)
     stretch = jnp.asarray(prolong_table(), BF16)
     turn = jnp.asarray(turn_table(), BF16)
-    n_z = n_row // 4
     dma = pltpu.SemaphoreType.DMA
     stage, total, outer = pl.pallas_call(
         functools.partial(
@@ -679,10 +656,10 @@
         ),
         out_shape=[
             jax.ShapeDtypeStruct((32, 32, 512), BF16),
-            jax.ShapeDtypeStruct((n_col, 24, 128), F32),
+            jax.ShapeDtypeStruct((192, 128), F32),
             jax.ShapeDtypeStruct((256, 128), F32),
         ],
-        in_specs=[hbm] * 2 + [pl.BlockSpec(memory_space=pltpu.SMEM)] + [hbm] * 10,
+        in_specs=[hbm] * 2 + [pl.BlockSpec(memory_space=pltpu.SMEM)] + [hbm] * 11,
         out_specs=[hbm, vmem, vmem],
         scratch_shapes=[
             pltpu.VMEM((32, 32, 512), BF16),
@@ -703,14 +680,14 @@
             pltpu.VMEM((10, 32, 512), F32),
             pltpu.VMEM((2, 128, 512), BF16),
             pltpu.SMEM(row_tab.shape[1:], F32),
+            pltpu.SMEM(back_tab.shape[1:], F32),
             pltpu.VMEM((64, 384), F32),
             pltpu.VMEM((n_col, 16, 384), F32),
-            pltpu.VMEM((n_row, 8, 128), F32),
-            pltpu.VMEM((n_z, 4, 8, 128), F32),
-            pltpu.VMEM((4, 8, 128), F32),
-            pltpu.VMEM((4, 8, 128), F32),
-            pltpu.VMEM((4, 8, 128), F32),
-            pltpu.VMEM((n_row, 8, 128), F32),
+            pltpu.VMEM((2, 16, 384), F32),
+            pltpu.VMEM((n_row // 2, 8, 128), F32),
+            pltpu.VMEM((n_row // 2, 8, 128), F32),
+            pltpu.VMEM((2, 4, 128), F32),
+            pltpu.VMEM((n_row, 4, 128), F32),
             pltpu.VMEM((16, 256), F32),
             pltpu.VMEM((n_col, 16, 256), F32),
             pltpu.VMEM((4, 1024), F32),
@@ -728,18 +705,18 @@
             pltpu.VMEM((3, 192, 256), BF16),
             pltpu.VMEM((3, 192, 256), F32),
             pltpu.VMEM((3, 192, 256), F32),
-            pltpu.VMEM((n_col, 24, 128), F32),
-            pltpu.VMEM((n_col, 24, 128), F32),
-            pltpu.VMEM((24, 128), F32),
-            pltpu.VMEM((4, 24, 128), F32),
-            pltpu.VMEM((24, 128), F32),
-            pltpu.VMEM((n_z, 24, 128), F32),
-            pltpu.VMEM((24, 128), F32),
-            pltpu.VMEM((n_col, 24, 128), F32),
-            dma((16,)),
+            pltpu.VMEM((2, n_col, 12, 128), F32),
+            pltpu.VMEM((n_col, 12, 128), F32),
+            pltpu.VMEM((n_col, 12, 128), F32),
+            pltpu.VMEM((n_col, 12, 128), F32),
+            pltpu.VMEM((12, 128), F32),
+            pltpu.VMEM((n_row // 2, 12, 128), F32),
+            pltpu.VMEM((12, 128), F32),
+            pltpu.VMEM((2, n_col, 12, 128), F32),
+            dma((17,)),
             dma((10,)),
             dma((10,)),
-            *[dma((7,))] * 20,
+            *[dma((16,))] * 22,
         ],
         compiler_params=pltpu.CompilerParams(
             collective_id=0, has_side_effects=True, vmem_limit_bytes=VMEM_LIMIT
@@ -747,7 +724,7 @@
         name="layer",
     )(
         features, mask, mask_gain, cotangent, spec_real, spec_imag, conv_one, conv_two,
-        spread, stretch, turn, col_tab, row_tab,
+        spread, stretch, turn, col_tab, row_tab, back_tab,
     )
     return pl.pallas_call(
         finish_kernel,
@@ -758,9 +735,8 @@
             jax.ShapeDtypeStruct((8, 32, 32), F32),
             jax.ShapeDtypeStruct((8, 32, 32), F32),
         ],
-        in_specs=[hbm, vmem, vmem],
-        out_specs=[hbm] + [vmem] * 4,
-        scratch_shapes=[pltpu.VMEM((32, 32, 512), BF16), dma((8,))],
+        in_specs=[vmem] * 3,
+        out_specs=[vmem] * 5,
         compiler_params=pltpu.CompilerParams(vmem_limit_bytes=VMEM_LIMIT),
         name="finish",
     )(stage, total, outer)

time: 59.4 us -> 50.9 us (0.86)
  Pallas kernels: 58.4 us -> 50.1 us
    pallas_call x1, Pallas kernels: 54.7 us -> 47.7 us  [body(): pl.pallas_call(functools.partial(main_kernel, n_row, n_col, scaling, 1.0...]
    pallas_call x1, Pallas kernels: 3.73 us -> 2.48 us  [body(): pl.pallas_call(finish_kernel, out_shape=[jax.ShapeDtypeStruct((32, 32, 51...]
where the time goes in v1:
time: 50.9 us; the launch traced here: 50.8 us
  Pallas kernels  50.1 us (98%)
  between operations  0.64 us (1%)
    pallas_call x1, Pallas kernels, body(): pl.pallas_call(functools.partial(main_kernel, n_row, n_col, scaling, 1.0...  47.7 us
    pallas_call x1, Pallas kernels, body(): pl.pallas_call(finish_kernel, out_shape=[jax.ShapeDtypeStruct((32, 32, 51...  2.48 us

profile of v1, /device:TPU:1, one launch (start us, length us, event | category | flops | bytes accessed | tf_op | source)
XLA Modules:
  0.0 50.8 jit_solution(8619733179934303197)
XLA Ops:
  0.6 47.7 %layer.1 = (bf16[32,32,512]{2,1,0:T(8,128)(2,1)}, f32[192,128]{1,0:T(8,128)}, f32[256,128]{1,0:T(8,128)}) custom-call(bf16[32,32,512]{2,1,0:T(8,128)(2,1)} %feat_h.1, s32[32,512]{1,0:T(8,128)} %mask_h.1, f32[32]{0:T(128)} %gain.1, bf16[32,32,512]{2,1,0:T(8,128)(2,1)} %cot_h.1, bf16[8,32,32]{2,1,0:T(8,128)(2,1)} %real_h.1, bf16[8,32,32]{2,1,0:T(8,128)(2,1)} %imag_h.1, ...), custom_call_target="tpu_custom_call" | custom-call | tf_op jit(solution)/shard_map/layer/pallas_call | solution.py:653
  48.3 2.5 %finish.1 = (bf16[32,32,512]{2,1,0:T(8,128)(2,1)}, f32[9,32,32]{2,1,0:T(8,128)}, f32[9,32,32]{2,1,0:T(8,128)}, f32[8,32,32]{2,1,0:T(8,128)}, f32[8,32,32]{2,1,0:T(8,128)}) custom-call(bf16[32,32,512]{2,1,0:T(8,128)(2,1)} %get-tuple-element.8.stage, f32[192,128]{1,0:T(8,128)} %get-tuple-element.9.total, f32[256,128]{1,0:T(8,128)} %get-tuple-element.10.outer), custom_call_target="tpu_custom_call" | custom-call | tf_op jit(solution)/shard_map/finish/pallas_call | solution.py:729

commit v2 on v1

--- a/solution.py
+++ b/solution.py
@@ -213,15 +213,14 @@
     n_row, n_col, scaling, scale,
     feat_h, mask_h, gain, cot_h, real_h, imag_h, one_h, two_h, spread_h, stretch_h, turn_h, col_tab, row_tab, back_tab,
     stage_out, total_out, outer_out,
-    feat, mask, cot, w_real, w_imag, w_one, w_two, spread, stretch, turn, stage,
+    feat, mask, cot, w_real, w_imag, w_one, w_two, spread, stretch, turn,
     lext, cext, high, low, field, tab, twiddle, twiddle_back,
     share, share_in, pair_in, part, part_in, duo, mixed_in, folded, folded_in,
     left, right, side_in, rows_in, row_c_in,
     l_shift, c_shift, h_shift, slope, band_one, band_two, band_tail, band_back, sum_one, sum_two,
-    mine, half_in, mine_half, sum_c, chunk, sum_g, done, gathered,
+    mine, sum_c, chunk, sum_g, done, gathered,
     local_sem, halo_send, halo_recv, a_send, a_recv, zp_send, zp_recv, b_send, b_recv, cp_send, cp_recv,
-    c_send, c_recv, d_send, d_recv, rp_send, rp_recv, r_send, r_recv, rg_send, rg_recv, g_send, g_recv,
-    gp_send, gp_recv,
+    c_send, c_recv, d_send, d_recv, r_send, r_recv, rg_send, rg_recv, g_send, g_recv,
 ):
     i = lax.axis_index("row")
     j = lax.axis_index("col")
@@ -235,6 +234,8 @@
     west, east = (j + n_col - 1) % n_col, (j + 1) % n_col
     cols = [(j + d) % n_col for d in range(1, n_col)]
     chips = [(chip + d) % n_chip for d in range(1, n_chip)]
+
+    flock = [(core, c) for c in cols] + [(other, c) for c in cols] + [(other, j)]
 
     def here(chip):
         return 2 * chip + core
@@ -268,6 +269,7 @@
         [(i, c) for c in cols]
         + [(here(g), j) for g in chips]
         + [(pair, j)]
+        + [(pair, c) for c in cols]
         + [(r, c) for r in (up, down) for c in (j, west, east)]
     )
     for partner in partners:
@@ -282,19 +284,6 @@
             load.wait()
 
     prepare(feat, mask, gain, cot, turn, lext, cext, field, (first_half, second_half))
-
-    loads[6].wait()
-    share[:, 0:128] = transform(tab[0], field[0:4].reshape(128, 512))
-    share[:, 128:320] = transform(tab[1], field[4:10].reshape(192, 512))
-    share[:, 320:384] = jnp.zeros((64, 64), F32)
-    pl.semaphore_wait(barrier, len(partners))
-
-    def group(c):
-        return pl.ds(pl.multiple_of(16 * (c % 4), 16), 16)
-
-    a_copies = remote_to([(share.at[group(c)], share_in.at[j], i, c) for c in cols], a_send, a_recv)
-    begin(a_copies)
-    share_in[j] = share[group(j), :]
 
     first_l = lext[4:36, :, 0:128].reshape(1024, 128)
     last_l = lext[4:36, :, 384:512].reshape(1024, 128)
@@ -307,6 +296,8 @@
     right[...] = (
         dot(pick(sel, ((0, 126), (1, 127))), last_l, NT) + dot(pick(sel, ((2, 127),)), last_c, NT)
     )[0:4]
+    pl.semaphore_wait(barrier, len(partners))
+
     plan = [
         (lext.at[4:6, :, 0:512], rows_in.at[1], up, j),
         (lext.at[34:36, :, 0:512], rows_in.at[0], down, j),
@@ -321,6 +312,18 @@
     ]
     halos = remote_to(plan, halo_send, halo_recv)
     begin(halos)
+
+    loads[6].wait()
+    share[:, 0:128] = transform(tab[0], field[0:4].reshape(128, 512))
+    share[:, 128:320] = transform(tab[1], field[4:10].reshape(192, 512))
+    share[:, 320:384] = jnp.zeros((64, 64), F32)
+
+    def group(c):
+        return pl.ds(pl.multiple_of(16 * (c % 4), 16), 16)
+
+    a_copies = remote_to([(share.at[group(c)], share_in.at[j], i, c) for c in cols], a_send, a_recv)
+    begin(a_copies)
+    share_in[j] = share[group(j), :]
 
     for load in loads[7:]:
         load.wait()
@@ -480,13 +483,9 @@
                 at = 96 * n + 32 * v + 4 * e
                 piece = at // 12
                 mine[piece // n_col, piece % n_col, at % 12 : at % 12 + 4, :] = total[4 * e : 4 * e + 4, 0:128]
-    rp_copies = remote_to([(mine.at[other], half_in, pair, j)], rp_send, rp_recv)
-    begin(rp_copies)
-    arrive(rp_copies)
-    mine_half[...] = mine[core] + half_in[...]
-    r_copies = remote_to([(mine_half.at[c], sum_c.at[j], i, c) for c in cols], r_send, r_recv)
+    r_copies = remote_to([(mine.at[b, c], sum_c.at[core, j], 2 * chip + b, c) for b, c in flock], r_send, r_recv)
     begin(r_copies)
-    sum_c[j] = mine_half[j]
+    sum_c[core, j] = mine[core, j]
 
     arrive(b_copies)
     spectrum = part_in[0]
@@ -537,9 +536,9 @@
     outer_out[...] = outer
 
     arrive(r_copies)
-    value = sum_c[0]
-    for k in range(1, n_col):
-        value = value + sum_c[k]
+    value = sum_c[0, 0]
+    for k in range(1, 2 * n_col):
+        value = value + sum_c[k // n_col, k % n_col]
     chunk[...] = value
     rg_copies = remote_to([(chunk, sum_g.at[chip], here(g), j) for g in chips], rg_send, rg_recv)
     begin(rg_copies)
@@ -576,7 +575,7 @@
         value = value + sum_g[k]
     value = value * scale
     done[...] = value
-    g_copies = remote_to([(done, gathered.at[core, j], i, c) for c in cols], g_send, g_recv)
+    g_copies = remote_to([(done, gathered.at[core, j], 2 * chip + b, c) for b, c in flock], g_send, g_recv)
     begin(g_copies)
     gathered[core, j] = value
     arrive(d_copies)
@@ -600,35 +599,25 @@
             total = total + dot(band_two[v], h_shift[v, 8 * t : 8 * t + 8].reshape(256, 512), NN)
         return total.reshape(32, 8, 512)
 
-    results = []
     for t in range(2):
         rows = slice(16 * t, 16 * t + 16)
         value = jnp.concatenate([window(2 * t), window(2 * t + 1)], axis=1)
-        stage[:, rows, :] = value.astype(BF16)
-        results.append(
-            pltpu.make_async_copy(stage.at[:, rows], stage_out.at[:, rows], local_sem.at[15 + t])
-        )
-        results[t].start()
+        stage_out[:, rows, :] = value.astype(BF16)
 
     for copies in (
-        a_copies, halos, zp_copies, b_copies, cp_copies, c_copies, d_copies, rp_copies, r_copies, rg_copies
+        a_copies, halos, zp_copies, b_copies, cp_copies, c_copies, d_copies, r_copies, rg_copies
     ):
         leave(copies)
     arrive(g_copies)
-    gp_copies = remote_to([(gathered.at[core], gathered.at[core], pair, j)], gp_send, gp_recv)
-    begin(gp_copies)
-    leave(g_copies)
-    for copy in results:
-        copy.wait()
-    arrive(gp_copies)
     for e in range(48):
         piece, at = divmod(4 * e, 12)
         total_out[4 * e : 4 * e + 4, :] = gathered[piece // n_col, piece % n_col, at : at + 4, :]
-    leave(gp_copies)
-
-
-def finish_kernel(stage, total, outer, out, out_one, out_two, g_real, g_imag):
-    out[...] = stage[...]
+    leave(g_copies)
+
+
+def finish_kernel(stage, total, outer, out, out_one, out_two, g_real, g_imag, sem):
+    copy = pltpu.make_async_copy(stage, out, sem)
+    copy.start()
     value = total[...]
     for n, grad in enumerate((out_one, out_two)):
         for v in range(3):
@@ -637,6 +626,7 @@
                 grad[3 * u + v] = value[at : at + 32, 32 * u : 32 * u + 32]
     g_real[...] = outer[:, 0:32].reshape(8, 32, 32)
     g_imag[...] = outer[:, 32:64].reshape(8, 32, 32)
+    copy.wait()
 
 
 def body(n_row, n_col, features, mask, mask_gain, conv_one, conv_two, spec_real, spec_imag, cotangent):
@@ -655,12 +645,12 @@
             main_kernel, n_row, n_col, scaling, 1.0 / math.sqrt(total_rows * total_cols)
         ),
         out_shape=[
-            jax.ShapeDtypeStruct((32, 32, 512), BF16),
-            jax.ShapeDtypeStruct((192, 128), F32),
-            jax.ShapeDtypeStruct((256, 128), F32),
+            pltpu.VMEM((32, 32, 512), BF16),
+            pltpu.VMEM((192, 128), F32),
+            pltpu.VMEM((256, 128), F32),
         ],
         in_specs=[hbm] * 2 + [pl.BlockSpec(memory_space=pltpu.SMEM)] + [hbm] * 11,
-        out_specs=[hbm, vmem, vmem],
+        out_specs=[vmem] * 3,
         scratch_shapes=[
             pltpu.VMEM((32, 32, 512), BF16),
             pltpu.VMEM((32, 512), jnp.int32),
@@ -672,7 +662,6 @@
             pltpu.VMEM(spread.shape, BF16),
             pltpu.VMEM(stretch.shape, BF16),
             pltpu.VMEM(turn.shape, BF16),
-            pltpu.VMEM((32, 32, 512), BF16),
             pltpu.VMEM((40, 32, 640), BF16),
             pltpu.VMEM((40, 32, 640), BF16),
             pltpu.VMEM((192, 512), BF16),
@@ -706,9 +695,7 @@
             pltpu.VMEM((3, 192, 256), F32),
             pltpu.VMEM((3, 192, 256), F32),
             pltpu.VMEM((2, n_col, 12, 128), F32),
-            pltpu.VMEM((n_col, 12, 128), F32),
-            pltpu.VMEM((n_col, 12, 128), F32),
-            pltpu.VMEM((n_col, 12, 128), F32),
+            pltpu.VMEM((2, n_col, 12, 128), F32),
             pltpu.VMEM((12, 128), F32),
             pltpu.VMEM((n_row // 2, 12, 128), F32),
             pltpu.VMEM((12, 128), F32),
@@ -716,7 +703,7 @@
             dma((17,)),
             dma((10,)),
             dma((10,)),
-            *[dma((16,))] * 22,
+            *[dma((16,))] * 18,
         ],
         compiler_params=pltpu.CompilerParams(
             collective_id=0, has_side_effects=True, vmem_limit_bytes=VMEM_LIMIT
@@ -736,10 +723,11 @@
             jax.ShapeDtypeStruct((8, 32, 32), F32),
         ],
         in_specs=[vmem] * 3,
-        out_specs=[vmem] * 5,
+        out_specs=[hbm] + [vmem] * 4,
+        scratch_shapes=[dma],
         compiler_params=pltpu.CompilerParams(vmem_limit_bytes=VMEM_LIMIT),
         name="finish",
-    )(stage, total, outer)
+    )(*(pltpu.with_memory_space_constraint(value, pltpu.VMEM) for value in (stage, total, outer)))
 
 
 def solution(mesh):

time: 50.9 us -> 47.3 us (0.929)
  Pallas kernels: 50.1 us -> 46.4 us
    pallas_call x1, Pallas kernels: 47.7 us -> 44.6 us  [body(): pl.pallas_call(functools.partial(main_kernel, n_row, n_col, scaling, 1.0...]
    pallas_call x1, Pallas kernels: 2.48 us -> 1.79 us  [body(): pl.pallas_call(finish_kernel, out_shape=[jax.ShapeDtypeStruct((32, 32, 51...]
where the time goes in v2:
time: 47.3 us; the launch traced here: 47.2 us
  Pallas kernels  46.4 us (98%)
  between operations  0.8 us (2%)
    pallas_call x1, Pallas kernels, body(): pl.pallas_call(functools.partial(main_kernel, n_row, n_col, scaling, 1.0...  44.6 us
    pallas_call x1, Pallas kernels, body(): pl.pallas_call(finish_kernel, out_shape=[jax.ShapeDtypeStruct((32, 32, 51...  1.79 us

profile of v2, /device:TPU:1, one launch (start us, length us, event | category | flops | bytes accessed | tf_op | source)
XLA Modules:
  0.0 47.2 jit_solution(9169093690065729793)
XLA Ops:
  0.6 44.6 %layer.1 = (bf16[32,32,512]{2,1,0:T(8,128)(2,1)S(1)}, f32[192,128]{1,0:T(8,128)S(1)}, f32[256,128]{1,0:T(8,128)S(1)}) custom-call(bf16[32,32,512]{2,1,0:T(8,128)(2,1)} %feat_h.1, s32[32,512]{1,0:T(8,128)} %mask_h.1, f32[32]{0:T(128)} %gain.1, bf16[32,32,512]{2,1,0:T(8,128)(2,1)} %cot_h.1, bf16[8,32,32]{2,1,0:T(8,128)(2,1)} %real_h.1, ...), custom_call_target="tpu_custom_call" | custom-call | tf_op jit(solution)/shard_map/layer/pallas_call | solution.py:643
  45.2 1.8 %finish.1 = (bf16[32,32,512]{2,1,0:T(8,128)(2,1)}, f32[9,32,32]{2,1,0:T(8,128)}, f32[9,32,32]{2,1,0:T(8,128)}, f32[8,32,32]{2,1,0:T(8,128)}, f32[8,32,32]{2,1,0:T(8,128)}) custom-call(bf16[32,32,512]{2,1,0:T(8,128)(2,1)S(1)} %get-tuple-element.8.stage, f32[192,128]{1,0:T(8,128)S(1)} %get-tuple-element.9.total, f32[256,128]{1,0:T(8,128)S(1)} %get-tuple-element.10.outer), custom_call_target="tpu_custom_call" | custom-call | tf_op jit(solution)/shard_map/finish/pallas_call | solution.py:716

commit v3 on v2

--- a/solution.py
+++ b/solution.py
@@ -204,8 +204,9 @@
 
 
 def shifted(value, by):
+    width = value.shape[1]
     if by > 0:
-        return jnp.concatenate([value[:, 640 - by :], value[:, : 640 - by]], axis=1)
+        return jnp.concatenate([value[:, width - by :], value[:, : width - by]], axis=1)
     return jnp.concatenate([value[:, -by:], value[:, :-by]], axis=1)
 
 
@@ -369,6 +370,13 @@
     pair_in[core] = total_a
     zp_copies = remote_to([(pair_in.at[core], pair_in.at[core], pair, j)], zp_send, zp_recv)
     begin(zp_copies)
+    for k in range(8):
+        rows = slice(4 + 4 * k, 8 + 4 * k)
+        for ref, shift in ((lext, l_shift), (cext, c_shift)):
+            value = ref[rows, :, 0:512].reshape(128, 512)
+            shift[0, rows, :, 0:512] = shifted(value, 1).reshape(4, 32, 512)
+            shift[1, rows, :, 0:512] = shifted(value, -1).reshape(4, 32, 512)
+
     arrive(halos)
     lext[2:4, :, 0:512] = rows_in[0]
     lext[36:38, :, 0:512] = rows_in[1]
@@ -380,17 +388,23 @@
     lext[:, :, 512:640] = dot(sides, at_l, TN).astype(BF16).reshape(40, 32, 128)
     cext[:, :, 512:640] = dot(sides, at_c, TN).astype(BF16).reshape(40, 32, 128)
 
-    def move(k):
-        rows = pl.ds(2 + 4 * k, 4)
-        value = lext[rows].reshape(128, 640)
-        l_shift[0, rows] = shifted(value, 1).reshape(4, 32, 640)
-        l_shift[1, rows] = shifted(value, -1).reshape(4, 32, 640)
-        value = cext[rows].reshape(128, 640)
-        c_shift[0, rows] = shifted(value, 1)[:, 0:512].reshape(4, 32, 512)
-        c_shift[1, rows] = shifted(value, -1)[:, 0:512].reshape(4, 32, 512)
-
-    for k in range(9):
-        move(k)
+    def column_tile(ref, rows, t):
+        return ref[rows, :, 128 * t : 128 * t + 128].reshape(-1, 128)
+
+    def joined(pieces):
+        return jnp.concatenate(pieces, axis=1).reshape(-1, 32, 128)
+
+    for ref, shift, rows in ((lext, l_shift, slice(2, 38)), (cext, c_shift, slice(3, 37))):
+        for row in (slice(rows.start, 4), slice(36, rows.stop)):
+            value = ref[row].reshape(-1, 640)
+            shift[0, row, :, 0:512] = shifted(value, 1)[:, 0:512].reshape(-1, 32, 512)
+            shift[1, row, :, 0:512] = shifted(value, -1)[:, 0:512].reshape(-1, 32, 512)
+        start, last, side = (column_tile(ref, rows, t) for t in (0, 3, 4))
+        shift[0, rows, :, 0:128] = joined([side[:, 127:128], start[:, 0:127]])
+        shift[1, rows, :, 384:512] = joined([last[:, 1:128], side[:, 0:1]])
+        if ref is lext:
+            shift[0, rows, :, 512:640] = joined([last[:, 127:128], side[:, 0:127]])
+            shift[1, rows, :, 512:640] = joined([side[:, 1:128], start[:, 0:1]])
 
     arrive(zp_copies)
     ps, qs = [], []
@@ -473,16 +487,19 @@
 
     for k in range(6):
         backward(k)
+    column = lax.broadcasted_iota(jnp.int32, (32, 128), 1)
     for n, sums in enumerate((sum_one, sum_two)):
         for v in range(3):
-            total = jnp.zeros((32, 256), F32)
-            for r in range(6):
-                value = sums[v, 32 * r : 32 * r + 32, :]
-                total = total + (pltpu.roll(value, 256 - 32 * r, 1) if r else value)
+            near = [sums[v, 32 * r : 32 * r + 32, 0:128] for r in range(4)]
+            far = [sums[v, 32 * r : 32 * r + 32, 128:256] for r in range(2, 6)]
+            total = near[0] + far[2]
+            total = total + pltpu.roll(near[1] + far[3], 96, 1)
+            total = total + pltpu.roll(jnp.where(column >= 64, near[2], far[0]), 64, 1)
+            total = total + pltpu.roll(jnp.where(column >= 96, near[3], far[1]), 32, 1)
             for e in range(8):
                 at = 96 * n + 32 * v + 4 * e
                 piece = at // 12
-                mine[piece // n_col, piece % n_col, at % 12 : at % 12 + 4, :] = total[4 * e : 4 * e + 4, 0:128]
+                mine[piece // n_col, piece % n_col, at % 12 : at % 12 + 4, :] = total[4 * e : 4 * e + 4, :]
     r_copies = remote_to([(mine.at[b, c], sum_c.at[core, j], 2 * chip + b, c) for b, c in flock], r_send, r_recv)
     begin(r_copies)
     sum_c[core, j] = mine[core, j]

time: 47.3 us -> 47.5 us (level)
  no operation moved by 1% of the time
where the time goes in v3:
time: 47.5 us; the launch traced here: 47.4 us
  Pallas kernels  46.6 us (98%)
  between operations  0.8 us (2%)
    pallas_call x1, Pallas kernels, body(): pl.pallas_call(functools.partial(main_kernel, n_row, n_col, scaling, 1.0...  44.8 us
    pallas_call x1, Pallas kernels, body(): pl.pallas_call(finish_kernel, out_shape=[jax.ShapeDtypeStruct((32, 32, 51...  1.79 us

profile of v3, /device:TPU:1, one launch (start us, length us, event | category | flops | bytes accessed | tf_op | source)
XLA Modules:
  0.0 47.4 jit_solution(15227837067488642592)
XLA Ops:
  0.6 44.8 %layer.1 = (bf16[32,32,512]{2,1,0:T(8,128)(2,1)S(1)}, f32[192,128]{1,0:T(8,128)S(1)}, f32[256,128]{1,0:T(8,128)S(1)}) custom-call(bf16[32,32,512]{2,1,0:T(8,128)(2,1)} %feat_h.1, s32[32,512]{1,0:T(8,128)} %mask_h.1, f32[32]{0:T(128)} %gain.1, bf16[32,32,512]{2,1,0:T(8,128)(2,1)} %cot_h.1, bf16[8,32,32]{2,1,0:T(8,128)(2,1)} %real_h.1, ...), custom_call_target="tpu_custom_call" | custom-call | tf_op jit(solution)/shard_map/layer/pallas_call | solution.py:660
  45.5 1.8 %finish.1 = (bf16[32,32,512]{2,1,0:T(8,128)(2,1)}, f32[9,32,32]{2,1,0:T(8,128)}, f32[9,32,32]{2,1,0:T(8,128)}, f32[8,32,32]{2,1,0:T(8,128)}, f32[8,32,32]{2,1,0:T(8,128)}) custom-call(bf16[32,32,512]{2,1,0:T(8,128)(2,1)S(1)} %get-tuple-element.8.stage, f32[192,128]{1,0:T(8,128)S(1)} %get-tuple-element.9.total, f32[256,128]{1,0:T(8,128)S(1)} %get-tuple-element.10.outer), custom_call_target="tpu_custom_call" | custom-call | tf_op jit(solution)/shard_map/finish/pallas_call | solution.py:733

commit v4 on v3

--- a/solution.py
+++ b/solution.py
@@ -436,7 +436,7 @@
             part[4 * l + b] = out
         return 0
 
-    lax.fori_loop(0, n_chip // 4, row_transform, 0)
+    lax.fori_loop(0, n_chip // 4, row_transform, 0, unroll=True)
     b_copies = remote_to([(part.at[g], part_in.at[chip], here(g), j) for g in chips], b_send, b_recv)
     begin(b_copies)
     part_in[chip] = part[chip]
@@ -570,7 +570,7 @@
                 sums[n] = sums[n] + twiddle_back[l, 16 * b + n] * value
         return tuple(sums)
 
-    sums = lax.fori_loop(0, n_row // 4, inverse, (jnp.zeros((4, 128), F32),) * 12)
+    sums = lax.fori_loop(0, n_row // 4, inverse, (jnp.zeros((4, 128), F32),) * 12, unroll=True)
     folded[:, 192:256] = jnp.zeros((16, 64), F32)
     grown = jnp.where((groups[0:4] < 2), twice[0:4], 2.0) * scaling
     even = groups[0:4] % 2 == 0

time: 47.5 us -> 47.1 us (level)
  no operation moved by 1% of the time
where the time goes in v4:
time: 47.1 us; the launch traced here: 47 us
  Pallas kernels  46.3 us (98%)
  between operations  0.64 us (1%)
    pallas_call x1, Pallas kernels, body(): pl.pallas_call(functools.partial(main_kernel, n_row, n_col, scaling, 1.0...  44.5 us
    pallas_call x1, Pallas kernels, body(): pl.pallas_call(finish_kernel, out_shape=[jax.ShapeDtypeStruct((32, 32, 51...  1.79 us

profile of v4, /device:TPU:1, one launch (start us, length us, event | category | flops | bytes accessed | tf_op | source)
XLA Modules:
  0.0 47.0 jit_solution(12817416480367419537)
XLA Ops:
  0.6 44.5 %layer.1 = (bf16[32,32,512]{2,1,0:T(8,128)(2,1)S(1)}, f32[192,128]{1,0:T(8,128)S(1)}, f32[256,128]{1,0:T(8,128)S(1)}) custom-call(bf16[32,32,512]{2,1,0:T(8,128)(2,1)} %feat_h.1, s32[32,512]{1,0:T(8,128)} %mask_h.1, f32[32]{0:T(128)} %gain.1, bf16[32,32,512]{2,1,0:T(8,128)(2,1)} %cot_h.1, bf16[8,32,32]{2,1,0:T(8,128)(2,1)} %real_h.1, ...), custom_call_target="tpu_custom_call" | custom-call | tf_op jit(solution)/shard_map/layer/pallas_call | solution.py:660
  45.2 1.8 %finish.1 = (bf16[32,32,512]{2,1,0:T(8,128)(2,1)}, f32[9,32,32]{2,1,0:T(8,128)}, f32[9,32,32]{2,1,0:T(8,128)}, f32[8,32,32]{2,1,0:T(8,128)}, f32[8,32,32]{2,1,0:T(8,128)}) custom-call(bf16[32,32,512]{2,1,0:T(8,128)(2,1)S(1)} %get-tuple-element.8.stage, f32[192,128]{1,0:T(8,128)S(1)} %get-tuple-element.9.total, f32[256,128]{1,0:T(8,128)S(1)} %get-tuple-element.10.outer), custom_call_target="tpu_custom_call" | custom-call | tf_op jit(solution)/shard_map/finish/pallas_call | solution.py:733
